TPU v7x, 32 devices: a whole 2x2x4 slice. The times are simulated.
32 devices in a mesh: parts: 2 (over x), rows: 16 (over z, y, core).
Axes of the slice: x: 2, y: 2, z: 4, core: 2. Of those that a mesh axis runs over, the one named last changes fastest.
Arguments:
- gain_tiles: float32 [4, 8192, 3, 128], P(None, ('parts', 'rows')), parts along dimension 1, may hold values from -0.21875 to 0.21875
- tile_pattern: int32 [8, 32, 3], P('parts'), parts along dimension 0, may hold values from 0 to 31, as said below
- offset_terms: float32 [4, 8192], P(None, ('parts', 'rows')), parts along dimension 1, may hold values from -6 to 6
- last_mean: float32 [8192], P(('parts', 'rows')), parts along dimension 0, may hold values from -6 to 6
- last_covariance: float32 [8192, 4096], P(('parts', 'rows')), parts along dimension 0, as said below
- noise_covariance: float32 [4, 8192, 4096], P(None, ('parts', 'rows')), parts along dimension 1, as said below
Outputs:
- smoothed_covariance: float32 [4, 8192, 4096], P(None, ('parts', 'rows')), parts along dimension 1
- smoothed_mean: float32 [4, 8192], P(None, ('parts', 'rows')), parts along dimension 1
There are 2 independent parts, one for each index of `parts`. A program takes and returns all parts, laid end to end along the dimension named above; each array names one. Nothing has to cross between parts.
Inputs may be any that keep to these rules, and one draw needn't show every extreme that they name: `tile_pattern`: each tile row names 3 different tile columns; the first is the tile row's own number. `last_covariance`: symmetric. `noise_covariance`: each block's matrix is symmetric.
All inputs are finite; a program needn't handle non-finite values.
Results may differ from a plain program's by a relative error of at most 0.0001.
Values sent between devices are 32-bit elements; how exact they have to be, the bound alone decides.
A program may use at most 192 MiB of HBM per device.

v0:
```python
import jax
import jax.numpy as jnp
from jax import lax
from jax.sharding import PartitionSpec as P

WIDTH = 4096
TILE = 128
PER_ROW = 3
BLOCKS = 4
TILE_ROWS = 32


def right_product(dense_rows, gain_values, pattern_block):
    row_count = dense_rows.shape[0]
    tiled = dense_rows.reshape(row_count, TILE_ROWS, TILE)
    picked = tiled[:, pattern_block, :]
    shaped = gain_values.reshape(TILE_ROWS, TILE, PER_ROW, TILE)
    result = jnp.einsum("rtkj,tckj->rtc", picked, shaped, precision=lax.Precision.HIGHEST)
    return result.reshape(row_count, WIDTH)


def left_product(columns, gain_values, pattern_block):
    column_count = columns.shape[1]
    tiled = columns.reshape(TILE_ROWS, TILE, column_count)
    picked = tiled[pattern_block]
    shaped = gain_values.reshape(TILE_ROWS, TILE, PER_ROW, TILE)
    result = jnp.einsum("tkjc,tqkj->ctq", picked, shaped, precision=lax.Precision.HIGHEST)
    return result.reshape(column_count, WIDTH)


def shards(gain_tiles, tile_pattern, offset_terms, last_mean, last_covariance, noise_covariance):
    local_rows = last_mean.shape[0]
    first_row = lax.axis_index("rows") * local_rows
    row_numbers = first_row + jnp.arange(local_rows, dtype=jnp.int32)
    tile_match = (
        row_numbers[:, None] // TILE == jnp.arange(TILE_ROWS, dtype=jnp.int32)[None, :]
    ).astype(jnp.int32)
    current_mean = last_mean
    covariance = last_covariance
    cov_list = []
    mean_list = []
    for block_index in reversed(range(BLOCKS)):
        pattern_block = tile_pattern[block_index]
        gain_values = lax.all_gather(gain_tiles[block_index], "rows", axis=0, tiled=True)
        partial_image = right_product(covariance, gain_values, pattern_block)
        received = lax.all_to_all(partial_image, "rows", split_axis=1, concat_axis=0, tiled=True)
        covariance = (
            left_product(received, gain_values, pattern_block) + noise_covariance[block_index]
        )
        cov_list.append(covariance)
        gathered_mean = lax.all_gather(current_mean, "rows", axis=0, tiled=True)
        mean_tiles = gathered_mean.reshape(TILE_ROWS, TILE)
        own_pattern = jnp.sum(tile_match[:, :, None] * pattern_block[None, :, :], axis=1)
        picked = mean_tiles[own_pattern]
        current_mean = (
            jnp.sum(picked * gain_tiles[block_index], axis=(1, 2)) + offset_terms[block_index]
        )
        mean_list.append(current_mean)
    cov_list = cov_list[::-1]
    mean_list = mean_list[::-1]
    return (jnp.stack(cov_list, 0), jnp.stack(mean_list, 0))


def solution(mesh):
    in_specs = (
        P(None, ("parts", "rows"), None, None),
        P("parts", None, None),
        P(None, ("parts", "rows")),
        P(("parts", "rows")),
        P(("parts", "rows"), None),
        P(None, ("parts", "rows"), None),
    )
    out_specs = (P(None, ("parts", "rows"), None), P(None, ("parts", "rows")))
    return jax.shard_map(shards, mesh=mesh, in_specs=in_specs, out_specs=out_specs, check_vma=False)
```

profile of v0, /device:TPU:0, one launch (start us, length us, event | category | flops | bytes accessed | tf_op | source)
XLA Modules:
  0.0 974.5 jit_solution(8600243610957248146)
XLA Ops:
  22.0 11.3 %gather_fusion = f32[96,256,128]{2,1,0:T(8,128)} fusion(f32[256,32,128]{2,0,1:T(8,128)} %copy.139, s32[1024]{0:T(1024)S(1)} %pad_clamp_fusion.7), kind=kCustom, calls=%fused_computation | custom fusion | bytes 25166208 | tf_op jit(solution)/shard_map/gather | solution.py:16
  33.3 41.6 %all-gather.13.cloned.1.call-done = f32[1,4096,3,128]{3,1,2,0:T(8,128)} async-done(((f32[1,256,3,128]{3,1,2,0:T(8,128)}), f32[1,4096,3,128]{3,1,2,0:T(8,128)}) %all-gather.13.cloned.1.call-update) | async-done | bytes 6291472 | tf_op jit(solution)/shard_map/all_gather | solution.py:44
  74.9 21.4 %fusion.17 = f32[32,256,128,1]{1,2,3,0:T(8,128)} fusion(f32[256,32,3,128]{3,0,2,1:T(8,128)} %bitcast.173, f32[32,128,3,128]{3,1,0,2:T(8,128)} %bitcast.184), kind=kOutput, calls=%fused_computation.30 | convolution fusion | flops 4831838208 | bytes 23068672 | tf_op jit(solution)/shard_map/rtkj,tckj->rtc/dot_general | solution.py:18
  122.6 97.4 %all-to-all-done = f32[256,16,256]{2,0,1:T(8,128)} async-done(((f32[256,16,256]{2,0,1:T(8,128)}), f32[256,16,256]{2,0,1:T(8,128)}, u32[]{:S(2)}, u32[]{:S(2)}) %all-to-all-start) | async-done | bytes 4194336 | tf_op jit(solution)/shard_map/all_to_all | solution.py:46
  231.1 15.4 %bitcast_add_fusion = (f32[256,32,128]{0,2,1:T(8,128)}, f32[32,256,128,1]{1,2,3,0:T(8,128)}) fusion(f32[256,32,128]{0,2,1:T(8,128)} %bitcast.190, f32[32,3,128,256]{3,2,1,0:T(8,128)} %bitcast.174, f32[32,128,3,128]{3,1,0,2:T(8,128)} %bitcast.185), kind=kOutput, calls=%fused_computation.32 | convolution fusion | flops 4832886784 | bytes 31457280 | tf_op jit(solution)/shard_map/tkjc,tqkj->ctq/dot_general | solution.py:27
  257.7 12.7 %copy.145 = f32[32,3,256,128]{3,2,1,0:T(8,128)} copy(f32[32,3,256,128]{2,3,1,0:T(8,128)} %bitcast.170) | data formatting | bytes 25165824 | tf_op jit(solution)/shard_map/gather | solution.py:16
  270.5 21.4 %fusion.4 = f32[32,256,128,1]{1,2,3,0:T(8,128)} fusion(f32[32,3,256,128]{3,2,1,0:T(8,128)} %copy.145, f32[32,128,3,128]{3,1,0,2:T(8,128)} %bitcast.182), kind=kOutput, calls=%fused_computation.17 | convolution fusion | flops 4831838208 | bytes 23068672 | tf_op jit(solution)/shard_map/rtkj,tckj->rtc/dot_general | solution.py:18
  297.3 40.2 %all-to-all-start.1 = ((f32[256,16,256]{2,0,1:T(8,128)}), f32[256,16,256]{2,0,1:T(8,128)}, u32[]{:S(2)}, u32[]{:S(2)}) async-start(f32[256,16,256]{2,0,1:T(8,128)} %copy.147), calls=%async_computation.1 | async-start | bytes 8388608 | tf_op jit(solution)/shard_map/all_to_all | solution.py:46
  344.1 108.9 %all-to-all-done.1 = f32[256,16,256]{2,0,1:T(8,128)} async-done(((f32[256,16,256]{2,0,1:T(8,128)}), f32[256,16,256]{2,0,1:T(8,128)}, u32[]{:S(2)}, u32[]{:S(2)}) %all-to-all-start.1) | async-done | bytes 4194336 | tf_op jit(solution)/shard_map/all_to_all | solution.py:46
  464.2 15.3 %bitcast_add_fusion.1 = (f32[256,32,128]{0,2,1:T(8,128)}, f32[32,256,128,1]{1,2,3,0:T(8,128)}) fusion(f32[256,32,128]{0,2,1:T(8,128)} %bitcast.191, f32[32,3,128,256]{3,2,1,0:T(8,128)} %bitcast.175, f32[32,128,3,128]{3,1,0,2:T(8,128)} %bitcast.183), kind=kOutput, calls=%fused_computation.33 | convolution fusion | flops 4832886784 | bytes 31457280 | tf_op jit(solution)/shard_map/tkjc,tqkj->ctq/dot_general | solution.py:27
  490.5 13.0 %copy.151 = f32[32,3,256,128]{3,2,1,0:T(8,128)} copy(f32[32,3,256,128]{2,3,1,0:T(8,128)} %bitcast.171) | data formatting | bytes 25165824 | tf_op jit(solution)/shard_map/gather | solution.py:16
  503.5 21.4 %fusion.2 = f32[32,256,128,1]{1,2,3,0:T(8,128)} fusion(f32[32,3,256,128]{3,2,1,0:T(8,128)} %copy.151, f32[32,128,3,128]{3,1,0,2:T(8,128)} %bitcast.180), kind=kOutput, calls=%fused_computation.15 | convolution fusion | flops 4831838208 | bytes 23068672 | tf_op jit(solution)/shard_map/rtkj,tckj->rtc/dot_general | solution.py:18
  530.3 19.9 %all-to-all-start.2 = ((f32[256,16,256]{2,0,1:T(8,128)}), f32[256,16,256]{2,0,1:T(8,128)}, u32[]{:S(2)}, u32[]{:S(2)}) async-start(f32[256,16,256]{2,0,1:T(8,128)} %copy.153), calls=%async_computation.2 | async-start | bytes 8388608 | tf_op jit(solution)/shard_map/all_to_all | solution.py:46
  556.1 71.8 %all-to-all-done.2 = f32[256,16,256]{2,0,1:T(8,128)} async-done(((f32[256,16,256]{2,0,1:T(8,128)}), f32[256,16,256]{2,0,1:T(8,128)}, u32[]{:S(2)}, u32[]{:S(2)}) %all-to-all-start.2) | async-done | bytes 4194336 | tf_op jit(solution)/shard_map/all_to_all | solution.py:46
  639.0 15.2 %bitcast_add_fusion.2 = (f32[256,32,128]{0,2,1:T(8,128)}, f32[32,256,128,1]{1,2,3,0:T(8,128)}) fusion(f32[256,32,128]{0,2,1:T(8,128)} %bitcast.189, f32[32,3,128,256]{3,2,1,0:T(8,128)} %bitcast.176, f32[32,128,3,128]{3,1,0,2:T(8,128)} %bitcast.181), kind=kOutput, calls=%fused_computation.34 | convolution fusion | flops 4832886784 | bytes 31457280 | tf_op jit(solution)/shard_map/tkjc,tqkj->ctq/dot_general | solution.py:27
  665.4 12.8 %copy.157 = f32[32,3,256,128]{3,2,1,0:T(8,128)} copy(f32[32,3,256,128]{2,3,1,0:T(8,128)} %bitcast.172) | data formatting | bytes 25165824 | tf_op jit(solution)/shard_map/gather | solution.py:16
  678.2 21.4 %fusion = f32[32,256,128,1]{1,2,3,0:T(8,128)} fusion(f32[32,3,256,128]{3,2,1,0:T(8,128)} %copy.157, f32[32,128,3,128]{3,1,0,2:T(8,128)} %bitcast.178), kind=kOutput, calls=%fused_computation.13 | convolution fusion | flops 4831838208 | bytes 23068672 | tf_op jit(solution)/shard_map/rtkj,tckj->rtc/dot_general | solution.py:18
  704.9 20.1 %all-to-all-start.3 = ((f32[256,16,256]{2,0,1:T(8,128)}), f32[256,16,256]{2,0,1:T(8,128)}, u32[]{:S(2)}, u32[]{:S(2)}) async-start(f32[256,16,256]{2,0,1:T(8,128)} %copy.159), calls=%async_computation.3 | async-start | bytes 8388608 | tf_op jit(solution)/shard_map/all_to_all | solution.py:46
  725.7 83.4 %all-gather.4 = f32[16,1,256]{2,1,0:T(1,128)S(1)} all-gather(f32[1,1,256]{2,1,0:T(1,128)S(1)} %bitcast.208), channel_id=1, replica_groups=mesh['parts'=2,'rows'=16] {'rows'}, dimensions={0}, use_global_device_ids=true | all-gather | bytes 17408 | tf_op jit(solution)/shard_map/all_gather | solution.py:51
  811.3 38.4 %all-gather.5 = f32[16,1,256]{2,1,0:T(1,128)S(1)} all-gather(f32[1,1,256]{2,1,0:T(1,128)S(1)} %bitcast.201), channel_id=1, replica_groups=mesh['parts'=2,'rows'=16] {'rows'}, dimensions={0}, use_global_device_ids=true | all-gather | bytes 17408 | tf_op jit(solution)/shard_map/all_gather | solution.py:51
  852.0 17.4 %all-gather.6 = f32[16,1,256]{2,1,0:T(1,128)S(1)} all-gather(f32[1,1,256]{2,1,0:T(1,128)S(1)} %bitcast.202), channel_id=1, replica_groups=mesh['parts'=2,'rows'=16] {'rows'}, dimensions={0}, use_global_device_ids=true | all-gather | bytes 17408 | tf_op jit(solution)/shard_map/all_gather | solution.py:51
  871.7 18.8 %all-gather.7 = f32[16,1,256]{2,1,0:T(1,128)S(1)} all-gather(f32[1,1,256]{2,1,0:T(1,128)S(1)} %bitcast.203), channel_id=1, replica_groups=mesh['parts'=2,'rows'=16] {'rows'}, dimensions={0}, use_global_device_ids=true | all-gather | bytes 17408 | tf_op jit(solution)/shard_map/all_gather | solution.py:51
  921.0 14.0 %fusion.6 = f32[32,256,128,1]{1,2,3,0:T(8,128)} fusion(f32[32,3,128,256]{3,2,1,0:T(8,128)} %bitcast.177, f32[32,128,3,128]{3,1,0,2:T(8,128)} %bitcast.179), kind=kOutput, calls=%fused_computation.19 | convolution fusion | flops 4831838208 | bytes 23068672 | tf_op jit(solution)/shard_map/tkjc,tqkj->ctq/dot_general | solution.py:27
  940.6 16.2 %slice_add_fusion = (f32[1,256,4096]{2,1,0:T(8,128)S(1)}, f32[1,256,4096]{2,1,0:T(8,128)}, f32[1,256,4096]{2,1,0:T(8,128)}, f32[1,256,4096]{2,1,0:T(8,128)}) fusion(f32[1,256,4096]{2,1,0:T(8,128)} %copy.161, f32[4,256,4096]{2,1,0:T(8,128)} %param.11, f32[1,256,4096]{2,1,0:T(8,128)} %copy.164, f32[1,256,4096]{2,1,0:T(8,128)} %copy.163, f32[1,256,4096]{2,1,0:T(8,128)} %copy.162), kind=kLoop, calls=%fused_computation.35 | loop fusion | flops 4194304 | bytes 50331648 | tf_op jit(solution)/shard_map/add | solution.py:48
  (99 shorter events, 190.3 us)
Async XLA Ops:
  7.2 67.7 %all-gather.13.cloned.1.call-start = ((), (), s32[]{:S(2)}) async-start(), calls=%async_computation.4 | async-start | bytes 6684672 | tf_op jit(solution)/shard_map/all_gather | solution.py:44
  9.8 260.7 %all-gather.15.cloned.1.call-start = ((), (), s32[]{:S(2)}) async-start(), calls=%async_computation.5 | async-start | bytes 6684672 | tf_op jit(solution)/shard_map/all_gather | solution.py:44
  16.1 5.6 copy-start.1
  101.7 118.3 %all-to-all-start = ((f32[256,16,256]{2,0,1:T(8,128)}), f32[256,16,256]{2,0,1:T(8,128)}, u32[]{:S(2)}, u32[]{:S(2)}) async-start(f32[256,16,256]{2,0,1:T(8,128)} %copy.141), calls=%async_computation | async-start | bytes 8388608 | tf_op jit(solution)/shard_map/all_to_all | solution.py:46
  106.2 397.3 %all-gather.17.cloned.1.call-start = ((), (), s32[]{:S(2)}) async-start(), calls=%async_computation.6 | async-start | bytes 6684672 | tf_op jit(solution)/shard_map/all_gather | solution.py:44
  297.3 155.8 %all-to-all-start.1 = ((f32[256,16,256]{2,0,1:T(8,128)}), f32[256,16,256]{2,0,1:T(8,128)}, u32[]{:S(2)}, u32[]{:S(2)}) async-start(f32[256,16,256]{2,0,1:T(8,128)} %copy.147), calls=%async_computation.1 | async-start | bytes 8388608 | tf_op jit(solution)/shard_map/all_to_all | solution.py:46
  337.5 340.6 %all-gather.19.cloned.1.call-start = ((), (), s32[]{:S(2)}) async-start(), calls=%async_computation.7 | async-start | bytes 6684672 | tf_op jit(solution)/shard_map/all_gather | solution.py:44
  530.3 97.6 %all-to-all-start.2 = ((f32[256,16,256]{2,0,1:T(8,128)}), f32[256,16,256]{2,0,1:T(8,128)}, u32[]{:S(2)}, u32[]{:S(2)}) async-start(f32[256,16,256]{2,0,1:T(8,128)} %copy.153), calls=%async_computation.2 | async-start | bytes 8388608 | tf_op jit(solution)/shard_map/all_to_all | solution.py:46
  704.9 20.1 %copy-start.2 = (s32[4,32,3]{1,0,2:T(4,128)S(1)}, s32[4,32,3]{1,0,2:T(4,128)}, u32[]{:S(2)}) copy-start(s32[4,32,3]{1,0,2:T(4,128)} %param.7) | copy-start | bytes 4612
  704.9 20.7 %copy-start.4 = (f32[256]{0:T(256)S(1)}, f32[256]{0:T(256)}, u32[]{:S(2)}) copy-start(f32[256]{0:T(256)} %param.9) | copy-start | bytes 3076
  704.9 106.2 %copy-start = (f32[4,256,3,128]{3,1,2,0:T(8,128)S(1)}, f32[4,256,3,128]{3,1,2,0:T(8,128)}, u32[]{:S(2)}) copy-start(f32[4,256,3,128]{3,1,2,0:T(8,128)} %param.6) | copy-start | bytes 4718596
  704.9 106.3 %copy-start.3 = (f32[4,256]{1,0:T(4,128)S(1)}, f32[4,256]{1,0:T(4,128)}, u32[]{:S(2)}) copy-start(f32[4,256]{1,0:T(4,128)} %param.8) | copy-start | bytes 12292
  704.9 205.0 %all-to-all-start.3 = ((f32[256,16,256]{2,0,1:T(8,128)}), f32[256,16,256]{2,0,1:T(8,128)}, u32[]{:S(2)}, u32[]{:S(2)}) async-start(f32[256,16,256]{2,0,1:T(8,128)} %copy.159), calls=%async_computation.3 | async-start | bytes 8388608 | tf_op jit(solution)/shard_map/all_to_all | solution.py:46
Sparse Core Ops, SparseCore 0:
  10.2 64.6 all-gather.12
  77.0 95.2 all-gather.14
  174.5 88.5 all-gather.16
  340.2 108.7 all-gather.18
where the time goes:
time: 979 us; the launch traced here: 974 us
  waiting for transfers between devices  321 us (33%)
  local copies, waits for them, and re-layouts  221 us (23%)
  blocking collectives  158 us (16%)
  matrix products  146 us (15%)
  starting transfers between devices  85.4 us (9%)
  other arithmetic  28.3 us (3%)
  between operations  14.6 us (1%)
    all_to_all x4, waiting for transfers between devices, shards(): lax.all_to_all(partial_image, 'rows', split_axis=1, concat_axis=0, tiled=...  278 us
    all_gather x4, blocking collectives, shards(): gathered_mean = lax.all_gather(current_mean, 'rows', axis=0, tiled=True)  158 us
    dot_general x4, matrix products, right_product(): jnp.einsum('rtkj,tckj->rtc', picked, shaped, precision=lax.Precision.HIGH...  85.7 us
    all_to_all x4, starting transfers between devices, shards(): lax.all_to_all(partial_image, 'rows', split_axis=1, concat_axis=0, tiled=...  84.8 us
    gather x7, local copies, waits for them, and re-layouts, right_product(): picked = tiled[:, pattern_block, :]  83.1 us
    dot_general x4, matrix products, left_product(): jnp.einsum('tkjc,tqkj->ctq', picked, shaped, precision=lax.Precision.HIGH...  59.8 us
    gather x4, local copies, waits for them, and re-layouts, left_product(): picked = tiled[pattern_block]  44.4 us
    all_gather x4, waiting for transfers between devices, shards(): lax.all_gather(gain_tiles[block_index], 'rows', axis=0, tiled=True)  41.7 us
  transfers between devices with their start and end apart: 8, of which 4 were waited for; matrix products, arithmetic and copies ran while one was open for 32% of the time, Pallas kernels for 0%

commit v1 on v0

--- a/solution.py
+++ b/solution.py
@@ -8,6 +8,27 @@
 PER_ROW = 3
 BLOCKS = 4
 TILE_ROWS = 32
+
+
+def joined_along(blocks, dim):
+    shape = list(blocks.shape[1:])
+    shape[dim] *= blocks.shape[0]
+    return jnp.moveaxis(blocks, 0, dim).reshape(shape)
+
+
+def doubled(value, axis):
+    size, index = (lax.axis_size(axis), lax.axis_index(axis))
+    blocks, bit = (value[None], 1)
+    while bit < size:
+        other = lax.ppermute(blocks, axis, [(i, i ^ bit) for i in range(size)])
+        low = index & bit == 0
+        blocks = jnp.concatenate([jnp.where(low, blocks, other), jnp.where(low, other, blocks)])
+        bit *= 2
+    return blocks
+
+
+def doubled_up(value, axis, dim):
+    return joined_along(doubled(value, axis), dim)
 
 
 def right_product(dense_rows, gain_values, pattern_block):
@@ -41,7 +62,7 @@
     mean_list = []
     for block_index in reversed(range(BLOCKS)):
         pattern_block = tile_pattern[block_index]
-        gain_values = lax.all_gather(gain_tiles[block_index], "rows", axis=0, tiled=True)
+        gain_values = doubled_up(gain_tiles[block_index], "rows", 0)
         partial_image = right_product(covariance, gain_values, pattern_block)
         received = lax.all_to_all(partial_image, "rows", split_axis=1, concat_axis=0, tiled=True)
         covariance = (

time: 979 us -> 1530 us (1.56)
  waiting for transfers between devices: 321 us -> 878 us
  other arithmetic: 28.3 us -> 69.1 us
  starting transfers between devices: 85.4 us -> 48.2 us
    ppermute x0 -> x16, waiting for transfers between devices: none -> 878 us  [doubled(): other = lax.ppermute(blocks, axis, [(i, i ^ bit) for i in range(size)])]
    all_to_all x4, waiting for transfers between devices: 278 us -> 0.01 us  [shards(): lax.all_to_all(partial_image, 'rows', split_axis=1, concat_axis=0, tiled=...]
    all_to_all x4, starting transfers between devices: 84.8 us -> 21.1 us  [shards(): lax.all_to_all(partial_image, 'rows', split_axis=1, concat_axis=0, tiled=...]
    all_gather x4 -> x0, waiting for transfers between devices: 41.7 us -> none  [shards(): lax.all_gather(gain_tiles[block_index], 'rows', axis=0, tiled=True)]
    ppermute x0 -> x16, starting transfers between devices: none -> 27.1 us  [doubled(): other = lax.ppermute(blocks, axis, [(i, i ^ bit) for i in range(size)])]
    select_n x0 -> x11, other arithmetic: none -> 20.7 us  [doubled(): jnp.where(low, blocks, other)]
    concatenate x0 -> x16, other arithmetic: none -> 19.4 us  [doubled(): jnp.concatenate([jnp.where(low, blocks, other), jnp.where(low, other, blo...]
  transfers between devices with their start and end apart: 8 -> 20, of which waited for: 4 -> 14; matrix products, arithmetic and copies ran while one was open for 32% -> 7% of each run, Pallas kernels for 0% -> 0%
where the time goes in v1:
time: 1530 us; the launch traced here: 1520 us
  waiting for transfers between devices  878 us (57%)
  local copies, waits for them, and re-layouts  226 us (15%)
  blocking collectives  158 us (10%)
  matrix products  142 us (9%)
  other arithmetic  69.1 us (5%)
  starting transfers between devices  48.2 us (3%)
    ppermute x16, waiting for transfers between devices, doubled(): other = lax.ppermute(blocks, axis, [(i, i ^ bit) for i in range(size)])  878 us
    all_gather x4, blocking collectives, shards(): gathered_mean = lax.all_gather(current_mean, 'rows', axis=0, tiled=True)  158 us
    dot_general x4, matrix products, right_product(): jnp.einsum('rtkj,tckj->rtc', picked, shaped, precision=lax.Precision.HIGH...  82.8 us
    gather x7, local copies, waits for them, and re-layouts, right_product(): picked = tiled[:, pattern_block, :]  82.8 us
    dot_general x4, matrix products, left_product(): jnp.einsum('tkjc,tqkj->ctq', picked, shaped, precision=lax.Precision.HIGH...  59 us
    gather x4, local copies, waits for them, and re-layouts, left_product(): picked = tiled[pattern_block]  44.4 us
  transfers between devices with their start and end apart: 20, of which 14 were waited for; matrix products, arithmetic and copies ran while one was open for 7% of the time, Pallas kernels for 0%

profile of v1, /device:TPU:0, one launch (start us, length us, event | category | flops | bytes accessed | tf_op | source)
XLA Modules:
  0.0 1522.8 jit_solution(10920920488856704714)
XLA Ops:
  15.7 17.6 %collective-permute-done.13 = f32[2,256,3,128]{3,1,0,2:T(8,128)S(1)} collective-permute-done((f32[2,256,3,128]{3,1,0,2:T(8,128)}, f32[2,256,3,128]{3,1,0,2:T(8,128)S(1)}, u32[]{:S(2)}, u32[]{:S(2)}) %collective-permute-start.13) | collective-permute-done | bytes 786464 | tf_op jit(solution)/shard_map/ppermute | solution.py:23
  33.3 16.4 %collective-permute-done.9 = f32[2,256,3,128]{3,1,0,2:T(8,128)S(1)} collective-permute-done((f32[2,256,3,128]{3,1,0,2:T(8,128)}, f32[2,256,3,128]{3,1,0,2:T(8,128)S(1)}, u32[]{:S(2)}, u32[]{:S(2)}) %collective-permute-start.9) | collective-permute-done | bytes 786464 | tf_op jit(solution)/shard_map/ppermute | solution.py:23
  53.9 34.2 %collective-permute-done.14 = f32[4,256,3,128]{3,1,0,2:T(8,128)} collective-permute-done((f32[4,256,3,128]{3,1,0,2:T(8,128)S(1)}, f32[4,256,3,128]{3,1,0,2:T(8,128)}, u32[]{:S(2)}, u32[]{:S(2)}) %collective-permute-start.14) | collective-permute-done | bytes 1572896 | tf_op jit(solution)/shard_map/ppermute | solution.py:23
  118.8 110.6 %collective-permute-done.15 = f32[8,256,3,128]{3,1,0,2:T(8,128)} collective-permute-done((f32[8,256,3,128]{3,1,0,2:T(8,128)}, f32[8,256,3,128]{3,1,0,2:T(8,128)}, u32[]{:S(2)}, u32[]{:S(2)}) %collective-permute-start.15) | collective-permute-done | bytes 3145760 | tf_op jit(solution)/shard_map/ppermute | solution.py:23
  232.3 19.2 %fusion.6 = f32[32,128,256,1]{2,1,0,3:T(8,128)} fusion(f32[32,128,3,128]{3,1,0,2:T(8,128)S(1)} %bitcast.204, f32[32,3,256,128]{3,2,1,0:T(8,128)} %bitcast.197), kind=kOutput, calls=%fused_computation.19 | convolution fusion | flops 4831838208 | bytes 23068672 | tf_op jit(solution)/shard_map/rtkj,tckj->rtc/dot_general | solution.py:39
  264.9 102.0 %collective-permute-done.10 = f32[4,256,3,128]{3,1,0,2:T(8,128)S(1)} collective-permute-done((f32[4,256,3,128]{3,1,0,2:T(8,128)S(1)}, f32[4,256,3,128]{3,1,0,2:T(8,128)S(1)}, u32[]{:S(2)}, u32[]{:S(2)}) %collective-permute-start.10) | collective-permute-done | bytes 1572896 | tf_op jit(solution)/shard_map/ppermute | solution.py:23
  389.8 118.9 %collective-permute-done.11 = f32[8,256,3,128]{3,1,0,2:T(8,128)} collective-permute-done((f32[8,256,3,128]{3,1,0,2:T(8,128)}, f32[8,256,3,128]{3,1,0,2:T(8,128)}, u32[]{:S(2)}, u32[]{:S(2)}) %collective-permute-start.11) | collective-permute-done | bytes 3145760 | tf_op jit(solution)/shard_map/ppermute | solution.py:23
  525.3 15.0 bitcast_add_fusion
  564.4 21.2 %fusion.4 = f32[32,128,256,1]{2,1,0,3:T(8,128)} fusion(f32[32,128,3,128]{3,1,0,2:T(8,128)} %bitcast.200, f32[32,3,256,128]{3,2,0,1:T(8,128)} %copy.155), kind=kOutput, calls=%fused_computation.17 | convolution fusion | flops 4831838208 | bytes 23068672 | tf_op jit(solution)/shard_map/rtkj,tckj->rtc/dot_general | solution.py:39
  598.3 51.8 %collective-permute-done.1 = f32[2,256,3,128]{3,1,0,2:T(8,128)S(1)} collective-permute-done((f32[2,256,3,128]{3,1,0,2:T(8,128)S(1)}, f32[2,256,3,128]{3,1,0,2:T(8,128)S(1)}, u32[]{:S(2)}, u32[]{:S(2)}) %collective-permute-start.1) | collective-permute-done | bytes 786464 | tf_op jit(solution)/shard_map/ppermute | solution.py:23
  650.1 27.6 %collective-permute-done.5 = f32[2,256,3,128]{3,1,0,2:T(8,128)S(1)} collective-permute-done((f32[2,256,3,128]{3,1,0,2:T(8,128)S(1)}, f32[2,256,3,128]{3,1,0,2:T(8,128)S(1)}, u32[]{:S(2)}, u32[]{:S(2)}) %collective-permute-start.5) | collective-permute-done | bytes 786464 | tf_op jit(solution)/shard_map/ppermute | solution.py:23
  679.3 35.9 %collective-permute-done.6 = f32[4,256,3,128]{3,1,0,2:T(8,128)S(1)} collective-permute-done((f32[4,256,3,128]{3,1,0,2:T(8,128)S(1)}, f32[4,256,3,128]{3,1,0,2:T(8,128)S(1)}, u32[]{:S(2)}, u32[]{:S(2)}) %collective-permute-start.6) | collective-permute-done | bytes 1572896 | tf_op jit(solution)/shard_map/ppermute | solution.py:23
  730.2 129.0 %collective-permute-done.7 = f32[8,256,3,128]{3,1,0,2:T(8,128)} collective-permute-done((f32[8,256,3,128]{3,1,0,2:T(8,128)}, f32[8,256,3,128]{3,1,0,2:T(8,128)}, u32[]{:S(2)}, u32[]{:S(2)}) %collective-permute-start.7) | collective-permute-done | bytes 3145760 | tf_op jit(solution)/shard_map/ppermute | solution.py:23
  875.9 15.1 bitcast_add_fusion.1
  914.9 21.2 %fusion.2 = f32[32,128,256,1]{2,1,0,3:T(8,128)} fusion(f32[32,128,3,128]{3,1,0,2:T(8,128)} %bitcast.202, f32[32,3,256,128]{3,2,0,1:T(8,128)} %copy.160), kind=kOutput, calls=%fused_computation.15 | convolution fusion | flops 4831838208 | bytes 23068672 | tf_op jit(solution)/shard_map/rtkj,tckj->rtc/dot_general | solution.py:39
  949.3 102.0 %collective-permute-done.2 = f32[4,256,3,128]{3,1,0,2:T(8,128)S(1)} collective-permute-done((f32[4,256,3,128]{3,1,0,2:T(8,128)S(1)}, f32[4,256,3,128]{3,1,0,2:T(8,128)S(1)}, u32[]{:S(2)}, u32[]{:S(2)}) %collective-permute-start.2) | collective-permute-done | bytes 1572896 | tf_op jit(solution)/shard_map/ppermute | solution.py:23
  1063.2 129.8 %collective-permute-done.3 = f32[8,256,3,128]{3,1,0,2:T(8,128)} collective-permute-done((f32[8,256,3,128]{3,1,0,2:T(8,128)}, f32[8,256,3,128]{3,1,0,2:T(8,128)}, u32[]{:S(2)}, u32[]{:S(2)}) %collective-permute-start.3) | collective-permute-done | bytes 3145760 | tf_op jit(solution)/shard_map/ppermute | solution.py:23
  1209.6 15.1 bitcast_add_fusion.2
  1248.5 21.2 %fusion = f32[32,128,256,1]{2,1,0,3:T(8,128)} fusion(f32[32,128,3,128]{3,1,0,2:T(8,128)} %bitcast.198, f32[32,3,256,128]{3,2,0,1:T(8,128)} %copy.165), kind=kOutput, calls=%fused_computation.13 | convolution fusion | flops 4831838208 | bytes 23068672 | tf_op jit(solution)/shard_map/rtkj,tckj->rtc/dot_general | solution.py:39
  1280.5 83.4 %all-gather = f32[16,1,256]{2,1,0:T(1,128)S(1)} all-gather(f32[1,1,256]{2,1,0:T(1,128)S(1)} %bitcast.232), channel_id=1, replica_groups=mesh['parts'=2,'rows'=16] {'rows'}, dimensions={0}, use_global_device_ids=true | all-gather | bytes 17408 | tf_op jit(solution)/shard_map/all_gather | solution.py:72
  1366.3 38.4 %all-gather.1 = f32[16,1,256]{2,1,0:T(1,128)S(1)} all-gather(f32[1,1,256]{2,1,0:T(1,128)S(1)} %bitcast.225), channel_id=1, replica_groups=mesh['parts'=2,'rows'=16] {'rows'}, dimensions={0}, use_global_device_ids=true | all-gather | bytes 17408 | tf_op jit(solution)/shard_map/all_gather | solution.py:72
  1407.0 17.4 %all-gather.2 = f32[16,1,256]{2,1,0:T(1,128)S(1)} all-gather(f32[1,1,256]{2,1,0:T(1,128)S(1)} %bitcast.226), channel_id=1, replica_groups=mesh['parts'=2,'rows'=16] {'rows'}, dimensions={0}, use_global_device_ids=true | all-gather | bytes 17408 | tf_op jit(solution)/shard_map/all_gather | solution.py:72
  1426.7 18.8 %all-gather.3 = f32[16,1,256]{2,1,0:T(1,128)S(1)} all-gather(f32[1,1,256]{2,1,0:T(1,128)S(1)} %bitcast.227), channel_id=1, replica_groups=mesh['parts'=2,'rows'=16] {'rows'}, dimensions={0}, use_global_device_ids=true | all-gather | bytes 17408 | tf_op jit(solution)/shard_map/all_gather | solution.py:72
  1495.4 16.3 %slice_add_fusion = (f32[1,256,4096]{2,1,0:T(8,128)S(1)}, f32[1,256,4096]{2,1,0:T(8,128)}, f32[1,256,4096]{2,1,0:T(8,128)}, f32[1,256,4096]{2,1,0:T(8,128)}) fusion(f32[1,256,4096]{2,1,0:T(8,128)} %copy.168, f32[4,256,4096]{2,1,0:T(8,128)} %param.11, f32[1,256,4096]{2,1,0:T(8,128)} %copy.171, f32[1,256,4096]{2,1,0:T(8,128)} %copy.170, f32[1,256,4096]{2,1,0:T(8,128)} %copy.169), kind=kLoop, calls=%fused_computation.37 | loop fusion | flops 4194304 | bytes 50331648 | tf_op jit(solution)/shard_map/add | solution.py:69
  (182 shorter events, 342.9 us)
Async XLA Ops:
  0.6 7.2 copy-start.1
  3.1 2.0 collective-permute-start
  3.6 2.7 collective-permute-start.12
  3.6 2.7 collective-permute-start.4
  4.1 3.7 collective-permute-start.8
  11.3 21.9 %collective-permute-start.13 = (f32[2,256,3,128]{3,1,0,2:T(8,128)}, f32[2,256,3,128]{3,1,0,2:T(8,128)S(1)}, u32[]{:S(2)}, u32[]{:S(2)}) collective-permute-start(f32[2,256,3,128]{3,1,0,2:T(8,128)} %pad_maximum_fusion.16), channel_id=1, source_target_pairs={{0,2},{1,3},{2,0},{3,1},{4,6},{5,7},{6,4},{7,5},{8,10},{9,11},{10,... | collective-permute-start | bytes 2359304 | tf_op jit(solution)/shard_map/ppermute | solution.py:23
  15.7 33.9 %collective-permute-start.9 = (f32[2,256,3,128]{3,1,0,2:T(8,128)}, f32[2,256,3,128]{3,1,0,2:T(8,128)S(1)}, u32[]{:S(2)}, u32[]{:S(2)}) collective-permute-start(f32[2,256,3,128]{3,1,0,2:T(8,128)} %pad_maximum_fusion.15), channel_id=1, source_target_pairs={{0,2},{1,3},{2,0},{3,1},{4,6},{5,7},{6,4},{7,5},{8,10},{9,11},{10,... | collective-permute-start | bytes 2359304 | tf_op jit(solution)/shard_map/ppermute | solution.py:23
  52.1 36.0 %collective-permute-start.14 = (f32[4,256,3,128]{3,1,0,2:T(8,128)S(1)}, f32[4,256,3,128]{3,1,0,2:T(8,128)}, u32[]{:S(2)}, u32[]{:S(2)}) collective-permute-start(f32[4,256,3,128]{3,1,0,2:T(8,128)S(1)} %pad_maximum_fusion.12), channel_id=1, source_target_pairs={{0,4},{1,5},{2,6},{3,7},{4,0},{5,1},{6,2},{7,3},{8,12},{9,13},{10,... | collective-permute-start | bytes 4718600 | tf_op jit(solution)/shard_map/ppermute | solution.py:23
  92.1 137.4 %collective-permute-start.15 = (f32[8,256,3,128]{3,1,0,2:T(8,128)}, f32[8,256,3,128]{3,1,0,2:T(8,128)}, u32[]{:S(2)}, u32[]{:S(2)}) collective-permute-start(f32[8,256,3,128]{3,1,0,2:T(8,128)} %pad_maximum_fusion.8), channel_id=1, source_target_pairs={{0,8},{1,9},{2,10},{3,11},{4,12},{5,13},{6,14},{7,15},{8,0},{9,1},... | collective-permute-start | bytes 9437192 | tf_op jit(solution)/shard_map/ppermute | solution.py:23
  232.3 19.2 %copy-start = (f32[16,256,3,128]{3,1,0,2:T(8,128)}, f32[16,256,3,128]{3,1,0,2:T(8,128)S(1)}, u32[]{:S(2)}) copy-start(f32[16,256,3,128]{3,1,0,2:T(8,128)S(1)} %pad_maximum_fusion.4) | copy-start | bytes 18874372
  256.9 257.3 %all-to-all-start = ((f32[256,16,256]{2,0,1:T(8,128)}), f32[256,16,256]{2,0,1:T(8,128)}, u32[]{:S(2)}, u32[]{:S(2)}) async-start(f32[256,16,256]{2,0,1:T(8,128)} %copy.151), calls=%async_computation | async-start | bytes 8388608 | tf_op jit(solution)/shard_map/all_to_all | solution.py:67
  262.8 104.1 %collective-permute-start.10 = (f32[4,256,3,128]{3,1,0,2:T(8,128)S(1)}, f32[4,256,3,128]{3,1,0,2:T(8,128)S(1)}, u32[]{:S(2)}, u32[]{:S(2)}) collective-permute-start(f32[4,256,3,128]{3,1,0,2:T(8,128)S(1)} %pad_maximum_fusion.11), channel_id=1, source_target_pairs={{0,4},{1,5},{2,6},{3,7},{4,0},{5,1},{6,2},{7,3},{8,12},{9,13},{10,... | collective-permute-start | bytes 4718600 | tf_op jit(solution)/shard_map/ppermute | solution.py:23
  370.4 138.3 %collective-permute-start.11 = (f32[8,256,3,128]{3,1,0,2:T(8,128)}, f32[8,256,3,128]{3,1,0,2:T(8,128)}, u32[]{:S(2)}, u32[]{:S(2)}) collective-permute-start(f32[8,256,3,128]{3,1,0,2:T(8,128)} %pad_maximum_fusion.7), channel_id=1, source_target_pairs={{0,8},{1,9},{2,10},{3,11},{4,12},{5,13},{6,14},{7,15},{8,0},{9,1},... | collective-permute-start | bytes 9437192 | tf_op jit(solution)/shard_map/ppermute | solution.py:23
  591.0 273.8 %all-to-all-start.1 = ((f32[256,16,256]{2,0,1:T(8,128)}), f32[256,16,256]{2,0,1:T(8,128)}, u32[]{:S(2)}, u32[]{:S(2)}) async-start(f32[256,16,256]{2,0,1:T(8,128)} %copy.156), calls=%async_computation.1 | async-start | bytes 8388608 | tf_op jit(solution)/shard_map/all_to_all | solution.py:67
  596.1 54.1 %collective-permute-start.1 = (f32[2,256,3,128]{3,1,0,2:T(8,128)S(1)}, f32[2,256,3,128]{3,1,0,2:T(8,128)S(1)}, u32[]{:S(2)}, u32[]{:S(2)}) collective-permute-start(f32[2,256,3,128]{3,1,0,2:T(8,128)S(1)} %pad_maximum_fusion.13), channel_id=1, source_target_pairs={{0,2},{1,3},{2,0},{3,1},{4,6},{5,7},{6,4},{7,5},{8,10},{9,11},{10,... | collective-permute-start | bytes 2359304 | tf_op jit(solution)/shard_map/ppermute | solution.py:23
  598.2 79.5 %collective-permute-start.5 = (f32[2,256,3,128]{3,1,0,2:T(8,128)S(1)}, f32[2,256,3,128]{3,1,0,2:T(8,128)S(1)}, u32[]{:S(2)}, u32[]{:S(2)}) collective-permute-start(f32[2,256,3,128]{3,1,0,2:T(8,128)S(1)} %pad_maximum_fusion.14), channel_id=1, source_target_pairs={{0,2},{1,3},{2,0},{3,1},{4,6},{5,7},{6,4},{7,5},{8,10},{9,11},{10,... | collective-permute-start | bytes 2359304 | tf_op jit(solution)/shard_map/ppermute | solution.py:23
  679.3 36.0 %collective-permute-start.6 = (f32[4,256,3,128]{3,1,0,2:T(8,128)S(1)}, f32[4,256,3,128]{3,1,0,2:T(8,128)S(1)}, u32[]{:S(2)}, u32[]{:S(2)}) collective-permute-start(f32[4,256,3,128]{3,1,0,2:T(8,128)S(1)} %pad_maximum_fusion.10), channel_id=1, source_target_pairs={{0,4},{1,5},{2,6},{3,7},{4,0},{5,1},{6,2},{7,3},{8,12},{9,13},{10,... | collective-permute-start | bytes 4718600 | tf_op jit(solution)/shard_map/ppermute | solution.py:23
  717.4 141.9 %collective-permute-start.7 = (f32[8,256,3,128]{3,1,0,2:T(8,128)}, f32[8,256,3,128]{3,1,0,2:T(8,128)}, u32[]{:S(2)}, u32[]{:S(2)}) collective-permute-start(f32[8,256,3,128]{3,1,0,2:T(8,128)} %pad_maximum_fusion.6), channel_id=1, source_target_pairs={{0,8},{1,9},{2,10},{3,11},{4,12},{5,13},{6,14},{7,15},{8,0},{9,1},... | collective-permute-start | bytes 9437192 | tf_op jit(solution)/shard_map/ppermute | solution.py:23
  941.5 257.0 %all-to-all-start.2 = ((f32[256,16,256]{2,0,1:T(8,128)}), f32[256,16,256]{2,0,1:T(8,128)}, u32[]{:S(2)}, u32[]{:S(2)}) async-start(f32[256,16,256]{2,0,1:T(8,128)} %copy.161), calls=%async_computation.2 | async-start | bytes 8388608 | tf_op jit(solution)/shard_map/all_to_all | solution.py:67
  947.2 104.1 %collective-permute-start.2 = (f32[4,256,3,128]{3,1,0,2:T(8,128)S(1)}, f32[4,256,3,128]{3,1,0,2:T(8,128)S(1)}, u32[]{:S(2)}, u32[]{:S(2)}) collective-permute-start(f32[4,256,3,128]{3,1,0,2:T(8,128)S(1)} %pad_maximum_fusion.9), channel_id=1, source_target_pairs={{0,4},{1,5},{2,6},{3,7},{4,0},{5,1},{6,2},{7,3},{8,12},{9,13},{10,... | collective-permute-start | bytes 4718600 | tf_op jit(solution)/shard_map/ppermute | solution.py:23
  1054.7 138.3 %collective-permute-start.3 = (f32[8,256,3,128]{3,1,0,2:T(8,128)}, f32[8,256,3,128]{3,1,0,2:T(8,128)}, u32[]{:S(2)}, u32[]{:S(2)}) collective-permute-start(f32[8,256,3,128]{3,1,0,2:T(8,128)} %pad_maximum_fusion.5), channel_id=1, source_target_pairs={{0,8},{1,9},{2,10},{3,11},{4,12},{5,13},{6,14},{7,15},{8,0},{9,1},... | collective-permute-start | bytes 9437192 | tf_op jit(solution)/shard_map/ppermute | solution.py:23
  1275.1 189.8 %all-to-all-start.3 = ((f32[256,16,256]{2,0,1:T(8,128)}), f32[256,16,256]{2,0,1:T(8,128)}, u32[]{:S(2)}, u32[]{:S(2)}) async-start(f32[256,16,256]{2,0,1:T(8,128)} %copy.166), calls=%async_computation.3 | async-start | bytes 8388608 | tf_op jit(solution)/shard_map/all_to_all | solution.py:67
  1279.9 86.3 %copy-start.2 = (f32[4,256,3,128]{3,1,2,0:T(8,128)S(1)}, f32[4,256,3,128]{3,1,2,0:T(8,128)}, u32[]{:S(2)}) copy-start(f32[4,256,3,128]{3,1,2,0:T(8,128)} %param.6) | copy-start | bytes 4718596
  1279.9 86.4 %copy-start.17 = (f32[4,256]{1,0:T(4,128)S(1)}, f32[4,256]{1,0:T(4,128)}, u32[]{:S(2)}) copy-start(f32[4,256]{1,0:T(4,128)} %param.8) | copy-start | bytes 12292
  (19 other events, 83.9 us)
